TPU v7x, 256 devices: a whole 4x4x8 slice. The times are simulated.
256 devices in a mesh: pairs: 32 (over y, z), tm: 8 (over x, core).
Axes of the slice: x: 4, y: 4, z: 8, core: 2. Of those that a mesh axis runs over, the one named last changes fastest.
Arguments:
- spectra: bfloat16 [8, 256, 2, 32768], P('tm', 'pairs'), may hold values from -6 to 6
- channel_slot: int32 [256], P('pairs'), may hold values from 0 to 7, as said below
- tile_list: int32 [63, 2], replicated, may hold values from 0 to 31, as said below
- tile_owner: int32 [63], replicated, may hold values from 0 to 31, as said below
Outputs:
- correlations: float32 [128, 64, 256], P('pairs', 'tm')
Inputs may be any that keep to these rules, and one draw needn't show every extreme that they name: `channel_slot`: within each block of 8 channels the values are a permutation of 0..7. `tile_list`: each row (i, j) has j = i or j = i + 1; every such pair of blocks appears exactly once, in some order. `tile_owner`: the owner of the tile in row p of tile_list is that row's i or i + 1; the tile of blocks 0 and 1 is owned by block 1; no owner holds more than 4 tiles, and some owner holds exactly 4.
All inputs are finite; a program needn't handle non-finite values.
Results may differ from a plain program's by a relative error of at most 0.00033.
Values may be sent and summed in bfloat16 or wider, within the bound.
A program may use at most 64 MiB of HBM per device.

v0:
```python
import math
import jax
import jax.numpy as jnp
from jax import lax
from jax.sharding import PartitionSpec as P

LAGS = 256
TILE_CAP = 4


def extended(block, sides, width):
    for axis, dim in sides:
        count = lax.axis_size(axis)
        forward = [(i, i + 1) for i in range(count - 1)]
        backward = [(target, source) for source, target in forward]
        low = lax.ppermute(
            lax.slice_in_dim(block, block.shape[dim] - width, None, axis=dim), axis, forward
        )
        high = lax.ppermute(lax.slice_in_dim(block, 0, width, axis=dim), axis, backward)
        block = jnp.concatenate([low, block, high], axis=dim)
    return block


def lag_table(freq_start, freq_width, bin_count, lag_count):
    freq_ids = freq_start + lax.iota(jnp.int32, freq_width)
    shift_lag = lax.iota(jnp.int32, lag_count) - lag_count // 2
    phase_steps = jnp.mod(freq_ids[:, None] * shift_lag[None, :], 2 * bin_count)
    phase_angle = phase_steps.astype(jnp.float32) * (math.pi / bin_count)
    cosine = jnp.cos(phase_angle).astype(jnp.bfloat16)
    sine_neg = (-jnp.sin(phase_angle)).astype(jnp.bfloat16)
    return jnp.concatenate([cosine, sine_neg], axis=0)


def cross_block(lead_block, tail_block):
    group_count = lead_block.shape[0]
    chan_count = lead_block.shape[1]
    lead_real = lead_block[:, :, 0].astype(jnp.float32)[:, :, None, :]
    lead_imag = lead_block[:, :, 1].astype(jnp.float32)[:, :, None, :]
    tail_real = tail_block[:, :, 0].astype(jnp.float32)[:, None, :, :]
    tail_imag = tail_block[:, :, 1].astype(jnp.float32)[:, None, :, :]
    real_part = lead_real * tail_real + lead_imag * tail_imag
    imag_part = lead_imag * tail_real - lead_real * tail_imag
    joined = jnp.concatenate(
        [real_part.astype(jnp.bfloat16), imag_part.astype(jnp.bfloat16)], axis=-1
    )
    return joined.reshape(group_count, chan_count * chan_count, joined.shape[-1])


def correlate(blocks, lead_pos, tail_pos, norm_scale):
    chan_count = blocks.shape[1]
    bin_count = blocks.shape[3]
    freq_width = min(2048, bin_count)
    slot_count = lead_pos.shape[0]

    def freq_turn(step_index, running):
        freq_start = step_index * freq_width
        freq_piece = lax.dynamic_slice_in_dim(blocks, freq_start, freq_width, 3)
        lead_block = jnp.take(freq_piece, lead_pos, axis=0)
        tail_block = jnp.take(freq_piece, tail_pos, axis=0)
        cross_spec = cross_block(lead_block, tail_block)
        lag_rows = lag_table(freq_start, freq_width, bin_count, LAGS)
        return running + jnp.einsum(
            "spf,fl->spl", cross_spec, lag_rows, preferred_element_type=jnp.float32
        )

    start_sum = jnp.zeros((slot_count, chan_count * chan_count, LAGS), jnp.float32)
    running = lax.fori_loop(0, bin_count // freq_width, freq_turn, start_sum)
    return running * norm_scale


def stack_windows(window_terms):
    summed = lax.psum(window_terms, "tm")
    share_rows = summed.shape[1] // lax.axis_size("tm")
    return lax.dynamic_slice_in_dim(summed, lax.axis_index("tm") * share_rows, share_rows, 1)


def on_device(spectra, channel_slot, tile_list, tile_owner):
    here_index = lax.axis_index("pairs")
    bin_count = spectra.shape[3]
    norm_scale = 1.0 / math.sqrt(2.0 * bin_count * lax.axis_size("tm"))
    ordered = jnp.take(spectra[0], channel_slot, axis=0)
    chan_count = ordered.shape[0]
    tile_count = tile_list.shape[0]
    low_block = tile_list[:, 0]
    high_block = tile_list[:, 1]
    earlier = lax.iota(jnp.int32, tile_count)[:, None] > lax.iota(jnp.int32, tile_count)[None, :]
    slot_rank = jnp.sum((tile_owner[:, None] == tile_owner[None, :]) & earlier, axis=1)
    slot_ids = lax.iota(jnp.int32, TILE_CAP)
    owned_slot = (
        (tile_owner[None, :] == here_index) & (slot_rank[None, :] == slot_ids[:, None])
    ).astype(jnp.int32)
    live_slot = jnp.sum(owned_slot, axis=1)
    slot_low = jnp.sum(owned_slot * low_block[None, :], axis=1)
    slot_high = jnp.sum(owned_slot * high_block[None, :], axis=1)
    widened = extended(ordered, (("pairs", 0),), chan_count)
    blocks = widened.reshape(3, chan_count, widened.shape[1], widened.shape[2])
    lead_pos = jnp.clip(slot_low - here_index + 1, 0, 2)
    tail_pos = jnp.clip(slot_high - here_index + 1, 0, 2)
    window_terms = correlate(blocks, lead_pos, tail_pos, norm_scale)
    window_terms = window_terms * live_slot[:, None, None].astype(jnp.float32)
    return stack_windows(window_terms)


def solution(mesh):
    placed = (P("tm", "pairs", None, None), P("pairs"), P(), P())
    return jax.shard_map(
        on_device, mesh=mesh, in_specs=placed, out_specs=P("pairs", "tm", None), check_vma=False
    )
```

profile of v0, /device:TPU:8, one launch (start us, length us, event | category | flops | bytes accessed | tf_op | source)
XLA Modules:
  0.0 379.8 jit_solution(1595996826397353993)
XLA Ops:
  8.0 2.7 gather_fusion.2
  11.6 7.7 %collective-permute-start.1 = (bf16[8,2,32768]{2,1,0:T(2,128)(2,1)S(1)}, bf16[8,2,32768]{2,1,0:T(2,128)(2,1)S(1)}, u32[]{:S(2)}, u32[]{:S(2)}) collective-permute-start(bf16[8,2,32768]{2,1,0:T(2,128)(2,1)S(1)} %broadcast_select_fusion.2), channel_id=1, source_target_pairs={{8,0},{16,8},{24,16},{32,24},{40,32},{48,40},{56,48},{64,56},{72,6... | collective-permute-start | bytes 3145736 | tf_op jit(solution)/shard_map/ppermute | solution.py:19
  19.3 1.9 collective-permute-start
  21.6 20.1 %collective-permute-done.1 = bf16[8,2,32768]{2,1,0:T(2,128)(2,1)S(1)} collective-permute-done((bf16[8,2,32768]{2,1,0:T(2,128)(2,1)S(1)}, bf16[8,2,32768]{2,1,0:T(2,128)(2,1)S(1)}, u32[]{:S(2)}, u32[]{:S(2)}) %collective-permute-start.1) | collective-permute-done | bytes 1048608 | tf_op jit(solution)/shard_map/ppermute | solution.py:19
  41.7 6.3 %collective-permute-done = bf16[8,2,32768]{2,1,0:T(2,128)(2,1)} collective-permute-done((bf16[8,2,32768]{2,1,0:T(2,128)(2,1)S(1)}, bf16[8,2,32768]{2,1,0:T(2,128)(2,1)}, u32[]{:S(2)}, u32[]{:S(2)}) %collective-permute-start) | collective-permute-done | bytes 1048608 | tf_op jit(solution)/shard_map/ppermute | solution.py:16
  48.0 7.1 %pad_maximum_fusion = bf16[24,2,32768]{2,1,0:T(2,128)(2,1)} fusion(bf16[8,2,32768]{2,1,0:T(2,128)(2,1)S(1)} %collective-permute-done.1, bf16[8,2,32768]{2,1,0:T(2,128)(2,1)S(1)} %broadcast_select_fusion.2, bf16[8,2,32768]{2,1,0:T(2,128)(2,1)} %collective-permute-done), kind=kLoop, calls=%fused_computation.45 | loop fusion | flops 3145728 | bytes 6291456 | tf_op jit(solution)/shard_map/concatenate | solution.py:20
  55.1 254.1 %while.16 = (s32[]{:T(128)}, f32[4,64,256]{2,1,0:T(8,128)S(1)}, bf16[3,8,2,32768]{3,2,1,0:T(2,128)(2,1)}, s32[4]{0:T(128)S(1)}, s32[4]{0:T(128)S(1)}, /*index=5*/s32[]{:T(128)}, s32[]{:T(128)}, s32[]{:T(128)}, s32[]{:T(128)}) while((s32[]{:T(128)}, f32[4,64,256]{2,1,0:T(8,128)S(1)}, bf16[3,8,2,32768]{3,2,1,0:T(2,128)(2,1)}, ...), condition=%wide.region_4.6_spmd.clone, body=%wide.region_3.5_spmd.clone.sunk | while | flops 559026496 | bytes 16148821 | solution.py:67
  60.7 9.4 %cosine_convert_fusion.2 = (bf16[2048,256]{1,0:T(8,128)(2,1)S(1)}, bf16[2048,256]{1,0:T(8,128)(2,1)S(1)}) fusion(s32[256]{0:T(256)S(1)} %iota_add_fusion.4, s32[2048]{0:T(1024)S(1)} %iota_add_fusion.5), kind=kLoop, calls=%fused_computation.19.clone.1 | loop fusion | flops 8912896 | bytes 2106368 | tf_op jit(solution)/shard_map/while/body/eval_jaxpr/convert_element_type | solution.py:29
  76.6 9.4 %cosine_convert_fusion.2 = (bf16[2048,256]{1,0:T(8,128)(2,1)S(1)}, bf16[2048,256]{1,0:T(8,128)(2,1)S(1)}) fusion(s32[256]{0:T(256)S(1)} %iota_add_fusion.4, s32[2048]{0:T(1024)S(1)} %iota_add_fusion.5), kind=kLoop, calls=%fused_computation.19.clone.1 | loop fusion | flops 8912896 | bytes 2106368 | tf_op jit(solution)/shard_map/while/body/eval_jaxpr/convert_element_type | solution.py:29
  92.5 9.4 %cosine_convert_fusion.2 = (bf16[2048,256]{1,0:T(8,128)(2,1)S(1)}, bf16[2048,256]{1,0:T(8,128)(2,1)S(1)}) fusion(s32[256]{0:T(256)S(1)} %iota_add_fusion.4, s32[2048]{0:T(1024)S(1)} %iota_add_fusion.5), kind=kLoop, calls=%fused_computation.19.clone.1 | loop fusion | flops 8912896 | bytes 2106368 | tf_op jit(solution)/shard_map/while/body/eval_jaxpr/convert_element_type | solution.py:29
  108.4 9.4 %cosine_convert_fusion.2 = (bf16[2048,256]{1,0:T(8,128)(2,1)S(1)}, bf16[2048,256]{1,0:T(8,128)(2,1)S(1)}) fusion(s32[256]{0:T(256)S(1)} %iota_add_fusion.4, s32[2048]{0:T(1024)S(1)} %iota_add_fusion.5), kind=kLoop, calls=%fused_computation.19.clone.1 | loop fusion | flops 8912896 | bytes 2106368 | tf_op jit(solution)/shard_map/while/body/eval_jaxpr/convert_element_type | solution.py:29
  124.2 9.4 %cosine_convert_fusion.2 = (bf16[2048,256]{1,0:T(8,128)(2,1)S(1)}, bf16[2048,256]{1,0:T(8,128)(2,1)S(1)}) fusion(s32[256]{0:T(256)S(1)} %iota_add_fusion.4, s32[2048]{0:T(1024)S(1)} %iota_add_fusion.5), kind=kLoop, calls=%fused_computation.19.clone.1 | loop fusion | flops 8912896 | bytes 2106368 | tf_op jit(solution)/shard_map/while/body/eval_jaxpr/convert_element_type | solution.py:29
  140.1 9.4 %cosine_convert_fusion.2 = (bf16[2048,256]{1,0:T(8,128)(2,1)S(1)}, bf16[2048,256]{1,0:T(8,128)(2,1)S(1)}) fusion(s32[256]{0:T(256)S(1)} %iota_add_fusion.4, s32[2048]{0:T(1024)S(1)} %iota_add_fusion.5), kind=kLoop, calls=%fused_computation.19.clone.1 | loop fusion | flops 8912896 | bytes 2106368 | tf_op jit(solution)/shard_map/while/body/eval_jaxpr/convert_element_type | solution.py:29
  156.0 9.4 %cosine_convert_fusion.2 = (bf16[2048,256]{1,0:T(8,128)(2,1)S(1)}, bf16[2048,256]{1,0:T(8,128)(2,1)S(1)}) fusion(s32[256]{0:T(256)S(1)} %iota_add_fusion.4, s32[2048]{0:T(1024)S(1)} %iota_add_fusion.5), kind=kLoop, calls=%fused_computation.19.clone.1 | loop fusion | flops 8912896 | bytes 2106368 | tf_op jit(solution)/shard_map/while/body/eval_jaxpr/convert_element_type | solution.py:29
  171.9 9.4 %cosine_convert_fusion.2 = (bf16[2048,256]{1,0:T(8,128)(2,1)S(1)}, bf16[2048,256]{1,0:T(8,128)(2,1)S(1)}) fusion(s32[256]{0:T(256)S(1)} %iota_add_fusion.4, s32[2048]{0:T(1024)S(1)} %iota_add_fusion.5), kind=kLoop, calls=%fused_computation.19.clone.1 | loop fusion | flops 8912896 | bytes 2106368 | tf_op jit(solution)/shard_map/while/body/eval_jaxpr/convert_element_type | solution.py:29
  187.8 9.4 %cosine_convert_fusion.2 = (bf16[2048,256]{1,0:T(8,128)(2,1)S(1)}, bf16[2048,256]{1,0:T(8,128)(2,1)S(1)}) fusion(s32[256]{0:T(256)S(1)} %iota_add_fusion.4, s32[2048]{0:T(1024)S(1)} %iota_add_fusion.5), kind=kLoop, calls=%fused_computation.19.clone.1 | loop fusion | flops 8912896 | bytes 2106368 | tf_op jit(solution)/shard_map/while/body/eval_jaxpr/convert_element_type | solution.py:29
  203.7 9.4 %cosine_convert_fusion.2 = (bf16[2048,256]{1,0:T(8,128)(2,1)S(1)}, bf16[2048,256]{1,0:T(8,128)(2,1)S(1)}) fusion(s32[256]{0:T(256)S(1)} %iota_add_fusion.4, s32[2048]{0:T(1024)S(1)} %iota_add_fusion.5), kind=kLoop, calls=%fused_computation.19.clone.1 | loop fusion | flops 8912896 | bytes 2106368 | tf_op jit(solution)/shard_map/while/body/eval_jaxpr/convert_element_type | solution.py:29
  219.5 9.4 %cosine_convert_fusion.2 = (bf16[2048,256]{1,0:T(8,128)(2,1)S(1)}, bf16[2048,256]{1,0:T(8,128)(2,1)S(1)}) fusion(s32[256]{0:T(256)S(1)} %iota_add_fusion.4, s32[2048]{0:T(1024)S(1)} %iota_add_fusion.5), kind=kLoop, calls=%fused_computation.19.clone.1 | loop fusion | flops 8912896 | bytes 2106368 | tf_op jit(solution)/shard_map/while/body/eval_jaxpr/convert_element_type | solution.py:29
  235.4 9.4 %cosine_convert_fusion.2 = (bf16[2048,256]{1,0:T(8,128)(2,1)S(1)}, bf16[2048,256]{1,0:T(8,128)(2,1)S(1)}) fusion(s32[256]{0:T(256)S(1)} %iota_add_fusion.4, s32[2048]{0:T(1024)S(1)} %iota_add_fusion.5), kind=kLoop, calls=%fused_computation.19.clone.1 | loop fusion | flops 8912896 | bytes 2106368 | tf_op jit(solution)/shard_map/while/body/eval_jaxpr/convert_element_type | solution.py:29
  251.3 9.4 %cosine_convert_fusion.2 = (bf16[2048,256]{1,0:T(8,128)(2,1)S(1)}, bf16[2048,256]{1,0:T(8,128)(2,1)S(1)}) fusion(s32[256]{0:T(256)S(1)} %iota_add_fusion.4, s32[2048]{0:T(1024)S(1)} %iota_add_fusion.5), kind=kLoop, calls=%fused_computation.19.clone.1 | loop fusion | flops 8912896 | bytes 2106368 | tf_op jit(solution)/shard_map/while/body/eval_jaxpr/convert_element_type | solution.py:29
  267.2 9.4 %cosine_convert_fusion.2 = (bf16[2048,256]{1,0:T(8,128)(2,1)S(1)}, bf16[2048,256]{1,0:T(8,128)(2,1)S(1)}) fusion(s32[256]{0:T(256)S(1)} %iota_add_fusion.4, s32[2048]{0:T(1024)S(1)} %iota_add_fusion.5), kind=kLoop, calls=%fused_computation.19.clone.1 | loop fusion | flops 8912896 | bytes 2106368 | tf_op jit(solution)/shard_map/while/body/eval_jaxpr/convert_element_type | solution.py:29
  283.1 9.4 %cosine_convert_fusion.2 = (bf16[2048,256]{1,0:T(8,128)(2,1)S(1)}, bf16[2048,256]{1,0:T(8,128)(2,1)S(1)}) fusion(s32[256]{0:T(256)S(1)} %iota_add_fusion.4, s32[2048]{0:T(1024)S(1)} %iota_add_fusion.5), kind=kLoop, calls=%fused_computation.19.clone.1 | loop fusion | flops 8912896 | bytes 2106368 | tf_op jit(solution)/shard_map/while/body/eval_jaxpr/convert_element_type | solution.py:29
  299.0 9.4 %cosine_convert_fusion.2 = (bf16[2048,256]{1,0:T(8,128)(2,1)S(1)}, bf16[2048,256]{1,0:T(8,128)(2,1)S(1)}) fusion(s32[256]{0:T(256)S(1)} %iota_add_fusion.4, s32[2048]{0:T(1024)S(1)} %iota_add_fusion.5), kind=kLoop, calls=%fused_computation.19.clone.1 | loop fusion | flops 8912896 | bytes 2106368 | tf_op jit(solution)/shard_map/while/body/eval_jaxpr/convert_element_type | solution.py:29
  310.0 61.6 %all-reduce.2.cloned.1.call-done = f32[4,64,256]{2,1,0:T(8,128)} async-done(((f32[4,64,256]{2,1,0:T(8,128)}), f32[4,64,256]{2,1,0:T(8,128)}) %all-reduce.2.cloned.1.call-update) | async-done | bytes 262160 | tf_op jit(solution)/shard_map/psum | solution.py:72
  (325 shorter events, 105.6 us)
Async XLA Ops:
  6.5 1.4 copy-start
  6.5 365.1 %all-reduce.2.cloned.1.call-start = ((), (), s32[]{:S(2)}) async-start(), calls=%async_computation | async-start | bytes 524288 | tf_op jit(solution)/shard_map/psum | solution.py:72
  8.0 13.3 %copy-start.2 = (s32[63]{0:T(128)S(1)}, s32[63]{0:T(128)}, u32[]{:S(2)}) copy-start(s32[63]{0:T(128)} %param.11) | copy-start | bytes 760
  8.0 13.5 %copy-start.1 = (s32[63,2]{0,1:T(2,128)S(1)}, s32[63,2]{0,1:T(2,128)}, u32[]{:S(2)}) copy-start(s32[63,2]{0,1:T(2,128)} %param.10) | copy-start | bytes 1516
  11.6 30.1 %collective-permute-start.1 = (bf16[8,2,32768]{2,1,0:T(2,128)(2,1)S(1)}, bf16[8,2,32768]{2,1,0:T(2,128)(2,1)S(1)}, u32[]{:S(2)}, u32[]{:S(2)}) collective-permute-start(bf16[8,2,32768]{2,1,0:T(2,128)(2,1)S(1)} %broadcast_select_fusion.2), channel_id=1, source_target_pairs={{8,0},{16,8},{24,16},{32,24},{40,32},{48,40},{56,48},{64,56},{72,6... | collective-permute-start | bytes 3145736 | tf_op jit(solution)/shard_map/ppermute | solution.py:19
  19.3 28.7 %collective-permute-start = (bf16[8,2,32768]{2,1,0:T(2,128)(2,1)S(1)}, bf16[8,2,32768]{2,1,0:T(2,128)(2,1)}, u32[]{:S(2)}, u32[]{:S(2)}) collective-permute-start(bf16[8,2,32768]{2,1,0:T(2,128)(2,1)S(1)} %broadcast_select_fusion.2), channel_id=1, source_target_pairs={{0,8},{8,16},{16,24},{24,32},{32,40},{40,48},{48,56},{56,64},{64,7... | collective-permute-start | bytes 3145736 | tf_op jit(solution)/shard_map/ppermute | solution.py:16
Sparse Core Ops, SparseCore 0:
  310.1 61.4 all-reduce.1
where the time goes:
time: 381 us; the launch traced here: 380 us
  other arithmetic  192 us (50%)
  waiting for transfers between devices  88 us (23%)
  local copies, waits for them, and re-layouts  60.9 us (16%)
  between operations  13.5 us (4%)
  matrix products  12.9 us (3%)
  starting transfers between devices  9.57 us (3%)
    convert_element_type x16, other arithmetic, lag_table(): cosine = jnp.cos(phase_angle).astype(jnp.bfloat16)  151 us
    psum x1, waiting for transfers between devices, stack_windows(): summed = lax.psum(window_terms, 'tm')  61.6 us
    ppermute x1, waiting for transfers between devices, extended(): lax.ppermute(lax.slice_in_dim(block, 0, width, axis=dim), axis, backward)  20.1 us
    gather x16, local copies, waits for them, and re-layouts, freq_turn(): tail_block = jnp.take(freq_piece, tail_pos, axis=0)  17.2 us
    gather x16, local copies, waits for them, and re-layouts, freq_turn(): lead_block = jnp.take(freq_piece, lead_pos, axis=0)  17.2 us
    dynamic_slice x16, local copies, waits for them, and re-layouts, freq_turn(): freq_piece = lax.dynamic_slice_in_dim(blocks, freq_start, freq_width, 3)  17.1 us
    dot_general x16, matrix products, freq_turn(): jnp.einsum('spf,fl->spl', cross_spec, lag_rows, preferred_element_type=jn...  12.9 us
    convert_element_type x16, other arithmetic, cross_block(): real_part.astype(jnp.bfloat16)  8.57 us
  transfers between devices with their start and end apart: 3, of which 3 were waited for; matrix products, arithmetic and copies ran while one was open for 0% of the time, Pallas kernels for 0%

commit v1 on v0

--- a/solution.py
+++ b/solution.py
@@ -69,7 +69,7 @@
 
 
 def stack_windows(window_terms):
-    summed = lax.psum(window_terms, "tm")
+    summed = jnp.sum(lax.all_gather(window_terms, "tm"), axis=0)
     share_rows = summed.shape[1] // lax.axis_size("tm")
     return lax.dynamic_slice_in_dim(summed, lax.axis_index("tm") * share_rows, share_rows, 1)
 

time: 381 us -> 346 us (0.908)
  waiting for transfers between devices: 88 us -> 50.8 us
    psum x1 -> x0, waiting for transfers between devices: 61.6 us -> none  [stack_windows(): summed = lax.psum(window_terms, 'tm')]
    all_gather x0 -> x1, waiting for transfers between devices: none -> 24.4 us  [stack_windows(): summed = jnp.sum(lax.all_gather(window_terms, 'tm'), axis=0)]
where the time goes in v1:
time: 346 us; the launch traced here: 344 us
  other arithmetic  195 us (56%)
  local copies, waits for them, and re-layouts  60.2 us (17%)
  waiting for transfers between devices  50.8 us (15%)
  between operations  13.5 us (4%)
  matrix products  13 us (4%)
  starting transfers between devices  9.57 us (3%)
    convert_element_type x16, other arithmetic, lag_table(): cosine = jnp.cos(phase_angle).astype(jnp.bfloat16)  151 us
    all_gather x1, waiting for transfers between devices, stack_windows(): summed = jnp.sum(lax.all_gather(window_terms, 'tm'), axis=0)  24.4 us
    ppermute x1, waiting for transfers between devices, extended(): lax.ppermute(lax.slice_in_dim(block, 0, width, axis=dim), axis, backward)  20.1 us
    gather x16, local copies, waits for them, and re-layouts, freq_turn(): lead_block = jnp.take(freq_piece, lead_pos, axis=0)  17.2 us
    gather x16, local copies, waits for them, and re-layouts, freq_turn(): tail_block = jnp.take(freq_piece, tail_pos, axis=0)  17.2 us
    dynamic_slice x16, local copies, waits for them, and re-layouts, freq_turn(): freq_piece = lax.dynamic_slice_in_dim(blocks, freq_start, freq_width, 3)  17.1 us
    dot_general x16, matrix products, freq_turn(): jnp.einsum('spf,fl->spl', cross_spec, lag_rows, preferred_element_type=jn...  13 us
    convert_element_type x16, other arithmetic, cross_block(): real_part.astype(jnp.bfloat16)  8.99 us
  transfers between devices with their start and end apart: 3, of which 3 were waited for; matrix products, arithmetic and copies ran while one was open for 0% of the time, Pallas kernels for 0%

profile of v1, /device:TPU:8, one launch (start us, length us, event | category | flops | bytes accessed | tf_op | source)
XLA Modules:
  0.0 344.0 jit_solution(2438151875269254930)
XLA Ops:
  8.0 2.7 gather_fusion.2
  11.6 7.7 %collective-permute-start.1 = (bf16[8,2,32768]{2,1,0:T(2,128)(2,1)S(1)}, bf16[8,2,32768]{2,1,0:T(2,128)(2,1)S(1)}, u32[]{:S(2)}, u32[]{:S(2)}) collective-permute-start(bf16[8,2,32768]{2,1,0:T(2,128)(2,1)S(1)} %broadcast_select_fusion.2), channel_id=1, source_target_pairs={{8,0},{16,8},{24,16},{32,24},{40,32},{48,40},{56,48},{64,56},{72,6... | collective-permute-start | bytes 3145736 | tf_op jit(solution)/shard_map/ppermute | solution.py:19
  19.3 1.9 collective-permute-start
  21.6 20.1 %collective-permute-done.1 = bf16[8,2,32768]{2,1,0:T(2,128)(2,1)S(1)} collective-permute-done((bf16[8,2,32768]{2,1,0:T(2,128)(2,1)S(1)}, bf16[8,2,32768]{2,1,0:T(2,128)(2,1)S(1)}, u32[]{:S(2)}, u32[]{:S(2)}) %collective-permute-start.1) | collective-permute-done | bytes 1048608 | tf_op jit(solution)/shard_map/ppermute | solution.py:19
  41.7 6.3 %collective-permute-done = bf16[8,2,32768]{2,1,0:T(2,128)(2,1)} collective-permute-done((bf16[8,2,32768]{2,1,0:T(2,128)(2,1)S(1)}, bf16[8,2,32768]{2,1,0:T(2,128)(2,1)}, u32[]{:S(2)}, u32[]{:S(2)}) %collective-permute-start) | collective-permute-done | bytes 1048608 | tf_op jit(solution)/shard_map/ppermute | solution.py:16
  48.0 7.1 %pad_maximum_fusion = bf16[24,2,32768]{2,1,0:T(2,128)(2,1)} fusion(bf16[8,2,32768]{2,1,0:T(2,128)(2,1)S(1)} %collective-permute-done.1, bf16[8,2,32768]{2,1,0:T(2,128)(2,1)S(1)} %broadcast_select_fusion.2, bf16[8,2,32768]{2,1,0:T(2,128)(2,1)} %collective-permute-done), kind=kLoop, calls=%fused_computation.45 | loop fusion | flops 3145728 | bytes 6291456 | tf_op jit(solution)/shard_map/concatenate | solution.py:20
  55.1 254.5 %while.16 = (s32[]{:T(128)}, f32[4,64,256]{2,1,0:T(8,128)S(1)}, bf16[3,8,2,32768]{3,2,1,0:T(2,128)(2,1)}, s32[4]{0:T(128)S(1)}, s32[4]{0:T(128)S(1)}, /*index=5*/s32[]{:T(128)}, s32[]{:T(128)}, s32[]{:T(128)}, s32[]{:T(128)}) while((s32[]{:T(128)}, f32[4,64,256]{2,1,0:T(8,128)S(1)}, bf16[3,8,2,32768]{3,2,1,0:T(2,128)(2,1)}, ...), condition=%wide.region_4.6_spmd.clone, body=%wide.region_3.5_spmd.clone.sunk | while | flops 559026496 | bytes 16148821 | solution.py:67
  60.7 9.4 %cosine_convert_fusion.2 = (bf16[2048,256]{1,0:T(8,128)(2,1)S(1)}, bf16[2048,256]{1,0:T(8,128)(2,1)S(1)}) fusion(s32[256]{0:T(256)S(1)} %iota_add_fusion.4, s32[2048]{0:T(1024)S(1)} %iota_add_fusion.5), kind=kLoop, calls=%fused_computation.19.clone.1 | loop fusion | flops 8912896 | bytes 2106368 | tf_op jit(solution)/shard_map/while/body/eval_jaxpr/convert_element_type | solution.py:29
  76.7 9.4 %cosine_convert_fusion.2 = (bf16[2048,256]{1,0:T(8,128)(2,1)S(1)}, bf16[2048,256]{1,0:T(8,128)(2,1)S(1)}) fusion(s32[256]{0:T(256)S(1)} %iota_add_fusion.4, s32[2048]{0:T(1024)S(1)} %iota_add_fusion.5), kind=kLoop, calls=%fused_computation.19.clone.1 | loop fusion | flops 8912896 | bytes 2106368 | tf_op jit(solution)/shard_map/while/body/eval_jaxpr/convert_element_type | solution.py:29
  92.6 9.4 %cosine_convert_fusion.2 = (bf16[2048,256]{1,0:T(8,128)(2,1)S(1)}, bf16[2048,256]{1,0:T(8,128)(2,1)S(1)}) fusion(s32[256]{0:T(256)S(1)} %iota_add_fusion.4, s32[2048]{0:T(1024)S(1)} %iota_add_fusion.5), kind=kLoop, calls=%fused_computation.19.clone.1 | loop fusion | flops 8912896 | bytes 2106368 | tf_op jit(solution)/shard_map/while/body/eval_jaxpr/convert_element_type | solution.py:29
  108.5 9.4 %cosine_convert_fusion.2 = (bf16[2048,256]{1,0:T(8,128)(2,1)S(1)}, bf16[2048,256]{1,0:T(8,128)(2,1)S(1)}) fusion(s32[256]{0:T(256)S(1)} %iota_add_fusion.4, s32[2048]{0:T(1024)S(1)} %iota_add_fusion.5), kind=kLoop, calls=%fused_computation.19.clone.1 | loop fusion | flops 8912896 | bytes 2106368 | tf_op jit(solution)/shard_map/while/body/eval_jaxpr/convert_element_type | solution.py:29
  124.4 9.4 %cosine_convert_fusion.2 = (bf16[2048,256]{1,0:T(8,128)(2,1)S(1)}, bf16[2048,256]{1,0:T(8,128)(2,1)S(1)}) fusion(s32[256]{0:T(256)S(1)} %iota_add_fusion.4, s32[2048]{0:T(1024)S(1)} %iota_add_fusion.5), kind=kLoop, calls=%fused_computation.19.clone.1 | loop fusion | flops 8912896 | bytes 2106368 | tf_op jit(solution)/shard_map/while/body/eval_jaxpr/convert_element_type | solution.py:29
  140.3 9.4 %cosine_convert_fusion.2 = (bf16[2048,256]{1,0:T(8,128)(2,1)S(1)}, bf16[2048,256]{1,0:T(8,128)(2,1)S(1)}) fusion(s32[256]{0:T(256)S(1)} %iota_add_fusion.4, s32[2048]{0:T(1024)S(1)} %iota_add_fusion.5), kind=kLoop, calls=%fused_computation.19.clone.1 | loop fusion | flops 8912896 | bytes 2106368 | tf_op jit(solution)/shard_map/while/body/eval_jaxpr/convert_element_type | solution.py:29
  156.2 9.4 %cosine_convert_fusion.2 = (bf16[2048,256]{1,0:T(8,128)(2,1)S(1)}, bf16[2048,256]{1,0:T(8,128)(2,1)S(1)}) fusion(s32[256]{0:T(256)S(1)} %iota_add_fusion.4, s32[2048]{0:T(1024)S(1)} %iota_add_fusion.5), kind=kLoop, calls=%fused_computation.19.clone.1 | loop fusion | flops 8912896 | bytes 2106368 | tf_op jit(solution)/shard_map/while/body/eval_jaxpr/convert_element_type | solution.py:29
  172.1 9.4 %cosine_convert_fusion.2 = (bf16[2048,256]{1,0:T(8,128)(2,1)S(1)}, bf16[2048,256]{1,0:T(8,128)(2,1)S(1)}) fusion(s32[256]{0:T(256)S(1)} %iota_add_fusion.4, s32[2048]{0:T(1024)S(1)} %iota_add_fusion.5), kind=kLoop, calls=%fused_computation.19.clone.1 | loop fusion | flops 8912896 | bytes 2106368 | tf_op jit(solution)/shard_map/while/body/eval_jaxpr/convert_element_type | solution.py:29
  188.0 9.4 %cosine_convert_fusion.2 = (bf16[2048,256]{1,0:T(8,128)(2,1)S(1)}, bf16[2048,256]{1,0:T(8,128)(2,1)S(1)}) fusion(s32[256]{0:T(256)S(1)} %iota_add_fusion.4, s32[2048]{0:T(1024)S(1)} %iota_add_fusion.5), kind=kLoop, calls=%fused_computation.19.clone.1 | loop fusion | flops 8912896 | bytes 2106368 | tf_op jit(solution)/shard_map/while/body/eval_jaxpr/convert_element_type | solution.py:29
  203.9 9.4 %cosine_convert_fusion.2 = (bf16[2048,256]{1,0:T(8,128)(2,1)S(1)}, bf16[2048,256]{1,0:T(8,128)(2,1)S(1)}) fusion(s32[256]{0:T(256)S(1)} %iota_add_fusion.4, s32[2048]{0:T(1024)S(1)} %iota_add_fusion.5), kind=kLoop, calls=%fused_computation.19.clone.1 | loop fusion | flops 8912896 | bytes 2106368 | tf_op jit(solution)/shard_map/while/body/eval_jaxpr/convert_element_type | solution.py:29
  219.8 9.4 %cosine_convert_fusion.2 = (bf16[2048,256]{1,0:T(8,128)(2,1)S(1)}, bf16[2048,256]{1,0:T(8,128)(2,1)S(1)}) fusion(s32[256]{0:T(256)S(1)} %iota_add_fusion.4, s32[2048]{0:T(1024)S(1)} %iota_add_fusion.5), kind=kLoop, calls=%fused_computation.19.clone.1 | loop fusion | flops 8912896 | bytes 2106368 | tf_op jit(solution)/shard_map/while/body/eval_jaxpr/convert_element_type | solution.py:29
  235.7 9.4 %cosine_convert_fusion.2 = (bf16[2048,256]{1,0:T(8,128)(2,1)S(1)}, bf16[2048,256]{1,0:T(8,128)(2,1)S(1)}) fusion(s32[256]{0:T(256)S(1)} %iota_add_fusion.4, s32[2048]{0:T(1024)S(1)} %iota_add_fusion.5), kind=kLoop, calls=%fused_computation.19.clone.1 | loop fusion | flops 8912896 | bytes 2106368 | tf_op jit(solution)/shard_map/while/body/eval_jaxpr/convert_element_type | solution.py:29
  251.6 9.4 %cosine_convert_fusion.2 = (bf16[2048,256]{1,0:T(8,128)(2,1)S(1)}, bf16[2048,256]{1,0:T(8,128)(2,1)S(1)}) fusion(s32[256]{0:T(256)S(1)} %iota_add_fusion.4, s32[2048]{0:T(1024)S(1)} %iota_add_fusion.5), kind=kLoop, calls=%fused_computation.19.clone.1 | loop fusion | flops 8912896 | bytes 2106368 | tf_op jit(solution)/shard_map/while/body/eval_jaxpr/convert_element_type | solution.py:29
  267.5 9.4 %cosine_convert_fusion.2 = (bf16[2048,256]{1,0:T(8,128)(2,1)S(1)}, bf16[2048,256]{1,0:T(8,128)(2,1)S(1)}) fusion(s32[256]{0:T(256)S(1)} %iota_add_fusion.4, s32[2048]{0:T(1024)S(1)} %iota_add_fusion.5), kind=kLoop, calls=%fused_computation.19.clone.1 | loop fusion | flops 8912896 | bytes 2106368 | tf_op jit(solution)/shard_map/while/body/eval_jaxpr/convert_element_type | solution.py:29
  283.4 9.4 %cosine_convert_fusion.2 = (bf16[2048,256]{1,0:T(8,128)(2,1)S(1)}, bf16[2048,256]{1,0:T(8,128)(2,1)S(1)}) fusion(s32[256]{0:T(256)S(1)} %iota_add_fusion.4, s32[2048]{0:T(1024)S(1)} %iota_add_fusion.5), kind=kLoop, calls=%fused_computation.19.clone.1 | loop fusion | flops 8912896 | bytes 2106368 | tf_op jit(solution)/shard_map/while/body/eval_jaxpr/convert_element_type | solution.py:29
  299.4 9.4 %cosine_convert_fusion.2 = (bf16[2048,256]{1,0:T(8,128)(2,1)S(1)}, bf16[2048,256]{1,0:T(8,128)(2,1)S(1)}) fusion(s32[256]{0:T(256)S(1)} %iota_add_fusion.4, s32[2048]{0:T(1024)S(1)} %iota_add_fusion.5), kind=kLoop, calls=%fused_computation.19.clone.1 | loop fusion | flops 8912896 | bytes 2106368 | tf_op jit(solution)/shard_map/while/body/eval_jaxpr/convert_element_type | solution.py:29
  310.5 24.4 %all-gather.3.cloned.1.call-done = f32[32,64,256]{2,1,0:T(8,128)} async-done(((f32[4,64,256]{2,1,0:T(8,128)}), f32[32,64,256]{2,1,0:T(8,128)}) %all-gather.3.cloned.1.call-update) | async-done | bytes 2097168 | tf_op jit(solution)/shard_map/all_gather | solution.py:72
  (326 shorter events, 107.1 us)
Async XLA Ops:
  6.5 1.4 copy-start
  6.5 328.3 %all-gather.3.cloned.1.call-start = ((), (), s32[]{:S(2)}) async-start(), calls=%async_computation | async-start | bytes 2359296 | tf_op jit(solution)/shard_map/all_gather | solution.py:72
  8.0 13.3 %copy-start.2 = (s32[63]{0:T(128)S(1)}, s32[63]{0:T(128)}, u32[]{:S(2)}) copy-start(s32[63]{0:T(128)} %param.11) | copy-start | bytes 760
  8.0 13.5 %copy-start.1 = (s32[63,2]{0,1:T(2,128)S(1)}, s32[63,2]{0,1:T(2,128)}, u32[]{:S(2)}) copy-start(s32[63,2]{0,1:T(2,128)} %param.10) | copy-start | bytes 1516
  11.6 30.1 %collective-permute-start.1 = (bf16[8,2,32768]{2,1,0:T(2,128)(2,1)S(1)}, bf16[8,2,32768]{2,1,0:T(2,128)(2,1)S(1)}, u32[]{:S(2)}, u32[]{:S(2)}) collective-permute-start(bf16[8,2,32768]{2,1,0:T(2,128)(2,1)S(1)} %broadcast_select_fusion.2), channel_id=1, source_target_pairs={{8,0},{16,8},{24,16},{32,24},{40,32},{48,40},{56,48},{64,56},{72,6... | collective-permute-start | bytes 3145736 | tf_op jit(solution)/shard_map/ppermute | solution.py:19
  19.3 28.7 %collective-permute-start = (bf16[8,2,32768]{2,1,0:T(2,128)(2,1)S(1)}, bf16[8,2,32768]{2,1,0:T(2,128)(2,1)}, u32[]{:S(2)}, u32[]{:S(2)}) collective-permute-start(bf16[8,2,32768]{2,1,0:T(2,128)(2,1)S(1)} %broadcast_select_fusion.2), channel_id=1, source_target_pairs={{0,8},{8,16},{16,24},{24,32},{32,40},{40,48},{48,56},{56,64},{64,7... | collective-permute-start | bytes 3145736 | tf_op jit(solution)/shard_map/ppermute | solution.py:16
Sparse Core Ops, SparseCore 0:
  310.6 24.1 all-gather.2
